TPU v7x, 32 devices: a whole 2x2x4 slice. The times are simulated.
32 devices in a mesh: region: 16 (over z, y, core), tracer: 2 (over x).
Axes of the slice: x: 2, y: 2, z: 4, core: 2. Of those that a mesh axis runs over, the one named last changes fastest.
Arguments:
- cotangent: float32 [32, 8192], P('tracer', 'region'), may hold values from -6 to 6
- states: float32 [6, 32, 8192], P(None, 'tracer', 'region'), may hold values from -6 to 6
- implicit_inverse: float32 [256, 32, 32], P('region'), may hold values from -3 to 3
- wet_levels: int32 [256], P('region'), may hold values from 1 to 32
- explicit_tiles: bfloat16 [16, 5, 512, 512], P('region'), may hold values from -0.125 to 0.125
- tile_offset: int32 [16, 5], P('region'), may hold values from -2 to 2, as said below
- tile_count: int32 [16], P('region'), may hold values from 1 to 5
- uptake_weight: float32 [32, 32], replicated, may hold values from -1 to 1
- release_weight: float32 [32, 32], replicated, may hold values from -1 to 1
Outputs:
- initial_adjoint: float32 [32, 8192], P('tracer', 'region')
Inputs may be any that keep to these rules, and one draw needn't show every extreme that they name: `tile_offset`: the offsets of one region are distinct; only the first tile_count slots of a region are used.
All inputs are finite; a program needn't handle non-finite values.
Results may differ from a plain program's by a relative error of at most 0.0032.
Values sent between devices are 32-bit elements; how exact they have to be, the bound alone decides.
A program may use at most 64 MiB of HBM per device.

v0:
```python
import jax
import jax.numpy as jnp
from jax import lax
from jax.sharding import PartitionSpec as P

REACH = 2


def from_behind(block, axis, distance):
    devices = range(lax.axis_size(axis))
    route = [((i - distance) % len(devices), i) for i in devices]
    return lax.ppermute(block, axis, route)


def reaction_terms(full_state, full_settled, uptake_weight, release_weight):
    highest = lax.Precision.HIGHEST
    uptake = jnp.dot(uptake_weight, full_state, precision=highest)
    pushed = jnp.dot(release_weight.T, full_settled, precision=highest)
    return (1.0 - jnp.tanh(uptake) ** 2) * pushed


def at_distance(offsets, tile_terms, distance):
    select = (offsets == distance).astype(jnp.float32)
    return jnp.sum(select[:, None, None] * tile_terms, axis=0)


def local(
    cotangent,
    states,
    implicit_inverse,
    wet_levels,
    explicit_tiles,
    tile_offset,
    tile_count,
    uptake_weight,
    release_weight,
):
    highest = lax.Precision.HIGHEST
    tr_dev, boxes = cotangent.shape
    columns, levels, _ = implicit_inverse.shape
    wet_mask = (
        (lax.broadcasted_iota(jnp.int32, (columns, levels), 1) < wet_levels[:, None])
        .astype(jnp.float32)
        .reshape(1, boxes)
    )
    tile_block = explicit_tiles[0]
    offsets = tile_offset[0]
    used_tiles = tile_count[0]
    slot_total = tile_block.shape[0]
    live_slots = (jnp.arange(slot_total, dtype=jnp.int32) < used_tiles).astype(jnp.float32)
    tracer_index = lax.axis_index("tracer")
    adjoint = cotangent
    for section in range(states.shape[0] - 1, -1, -1):
        settled = (
            jnp.einsum(
                "tcm,cml->tcl",
                adjoint.reshape(tr_dev, columns, levels),
                implicit_inverse,
                precision=highest,
            ).reshape(tr_dev, boxes)
            * wet_mask
        )
        settled_half = settled.astype(jnp.bfloat16)
        tile_terms = (
            jnp.einsum("tb,kbc->ktc", settled_half, tile_block, preferred_element_type=jnp.float32)
            * live_slots[:, None, None]
        )
        inflow = at_distance(offsets, tile_terms, 0)
        for offset in range(-REACH, REACH + 1):
            if offset != 0:
                outgoing = at_distance(offsets, tile_terms, offset)
                inflow = inflow + from_behind(outgoing, "region", offset)
        state = states[section]
        full_state, full_settled = (
            lax.all_gather(state, "tracer", axis=0, tiled=True),
            lax.all_gather(settled, "tracer", axis=0, tiled=True),
        )
        weighted = reaction_terms(full_state, full_settled, uptake_weight, release_weight)
        own_rows = lax.dynamic_slice_in_dim(uptake_weight, tracer_index * tr_dev, tr_dev, 1)
        reacted = jnp.dot(own_rows.T, weighted, precision=highest)
        adjoint = wet_mask * (inflow + reacted)
    return adjoint


def solution(mesh):
    placed = (
        P("tracer", "region"),
        P(None, "tracer", "region"),
        P("region", None, None),
        P("region"),
        P("region", None, None, None),
        P("region", None),
        P("region"),
        P(),
        P(),
    )
    return jax.shard_map(
        local, mesh=mesh, in_specs=placed, out_specs=P("tracer", "region"), check_vma=False
    )
```

profile of v0, /device:TPU:0, one launch (start us, length us, event | category | flops | bytes accessed | tf_op | source)
XLA Modules:
  0.0 125.3 jit_solution(9422949040306601059)
XLA Ops:
  0.0 0.8 fusion.85
  0.8 0.8 fusion.84
  1.6 0.8 reshape.146
  2.5 1.3 %multiply_convert_fusion.5 = (bf16[16,16,32]{2,0,1:T(8,128)(2,1)S(1)}, f32[16,16,32]{2,0,1:T(8,128)S(1)}) fusion(f32[16,32]{1,0:T(8,128)S(1)} %fusion.84, f32[16,32,32]{2,1,0:T(8,128)} %param.11, f32[16,16,32]{2,1,0:T(8,128)S(1)} %reshape.146), kind=kOutput, calls=%fused_computation.95 | convolution fusion | flops 3162112 | bytes 149504 | tf_op jit(solution)/shard_map/tcm,cml->tcl/dot_general | solution.py:55
  4.6 1.1 multiply_reduce_fusion.28
  5.7 6.0 %collective-permute-start = (f32[16,512]{1,0:T(8,128)}, f32[16,512]{1,0:T(8,128)}, u32[]{:S(2)}, u32[]{:S(2)}) collective-permute-start(f32[16,512]{1,0:T(8,128)} %get-tuple-element.30), channel_id=1, source_target_pairs={{4,0},{6,2},{8,4},{10,6},{12,8},{14,10},{16,12},{18,14},{20,16},{2... | collective-permute-start | bytes 98312 | tf_op jit(solution)/shard_map/ppermute | solution.py:12
  11.8 0.5 collective-permute-start.2
  12.3 0.7 collective-permute-start.3
  13.2 4.6 %all_gather.37 = f32[32,512]{1,0:T(8,128)S(1)} all-gather(f32[16,512]{1,0:T(8,128)S(1)} %broadcast_multiply_fusion.5), channel_id=1, replica_groups=mesh['region'=16,'tracer'=2] {'tracer'}, dimensions={0}, use_global_device_ids=true | all-gather | bytes 98304 | tf_op jit(solution)/shard_map/all_gather | solution.py:76
  17.8 4.6 %all-gather = f32[1,32,512]{2,1,0:T(8,128)S(1)} all-gather(f32[1,16,512]{2,1,0:T(8,128)S(1)} %get-tuple-element.39), channel_id=2, replica_groups=mesh['region'=16,'tracer'=2] {'tracer'}, dimensions={1}, use_global_device_ids=true | all-gather | bytes 98304 | tf_op jit(solution)/shard_map/all_gather | solution.py:75
  22.4 4.6 %all-gather.1 = f32[1,32,512]{2,1,0:T(8,128)S(1)} all-gather(f32[1,16,512]{2,1,0:T(8,128)S(1)} %get-tuple-element.38), channel_id=3, replica_groups=mesh['region'=16,'tracer'=2] {'tracer'}, dimensions={1}, use_global_device_ids=true | all-gather | bytes 98304 | tf_op jit(solution)/shard_map/all_gather | solution.py:75
  27.4 4.7 %all-gather.2 = f32[1,32,512]{2,1,0:T(8,128)S(1)} all-gather(f32[1,16,512]{2,1,0:T(8,128)S(1)} %get-tuple-element.37), channel_id=4, replica_groups=mesh['region'=16,'tracer'=2] {'tracer'}, dimensions={1}, use_global_device_ids=true | all-gather | bytes 98304 | tf_op jit(solution)/shard_map/all_gather | solution.py:75
  32.3 4.6 %all-gather.3 = f32[1,32,512]{2,1,0:T(8,128)S(1)} all-gather(f32[1,16,512]{2,1,0:T(8,128)S(1)} %get-tuple-element.36), channel_id=5, replica_groups=mesh['region'=16,'tracer'=2] {'tracer'}, dimensions={1}, use_global_device_ids=true | all-gather | bytes 98304 | tf_op jit(solution)/shard_map/all_gather | solution.py:75
  37.1 4.6 %all-gather.4 = f32[1,32,512]{2,1,0:T(8,128)S(1)} all-gather(f32[1,16,512]{2,1,0:T(8,128)S(1)} %get-tuple-element.40), channel_id=6, replica_groups=mesh['region'=16,'tracer'=2] {'tracer'}, dimensions={1}, use_global_device_ids=true | all-gather | bytes 98304 | tf_op jit(solution)/shard_map/all_gather | solution.py:75
  41.9 4.6 %all-gather.5 = f32[1,32,512]{2,1,0:T(8,128)S(1)} all-gather(f32[1,16,512]{2,1,0:T(8,128)S(1)} %get-tuple-element.35), channel_id=7, replica_groups=mesh['region'=16,'tracer'=2] {'tracer'}, dimensions={1}, use_global_device_ids=true | all-gather | bytes 98304 | tf_op jit(solution)/shard_map/all_gather | solution.py:75
  47.0 1.1 add_multiply_fusion.5
  48.9 4.6 %all_gather.39 = f32[32,512]{1,0:T(8,128)S(1)} all-gather(f32[16,512]{1,0:T(8,128)S(1)} %broadcast_multiply_fusion.4), channel_id=1, replica_groups=mesh['region'=16,'tracer'=2] {'tracer'}, dimensions={0}, use_global_device_ids=true | all-gather | bytes 98304 | tf_op jit(solution)/shard_map/all_gather | solution.py:76
  53.6 1.2 multiply_reduce_fusion.23
  54.8 4.1 %collective-permute-start.4 = (f32[16,512]{1,0:T(8,128)S(1)}, f32[16,512]{1,0:T(8,128)S(1)}, u32[]{:S(2)}, u32[]{:S(2)}) collective-permute-start(f32[16,512]{1,0:T(8,128)S(1)} %get-tuple-element.25), channel_id=1, source_target_pairs={{4,0},{6,2},{8,4},{10,6},{12,8},{14,10},{16,12},{18,14},{20,16},{2... | collective-permute-start | bytes 98312 | tf_op jit(solution)/shard_map/ppermute | solution.py:12
  58.9 0.5 collective-permute-start.6
  59.6 0.8 collective-permute-done.4
  60.8 4.1 %collective-permute-done.6 = f32[16,512]{1,0:T(8,128)S(1)} collective-permute-done((f32[16,512]{1,0:T(8,128)S(1)}, f32[16,512]{1,0:T(8,128)S(1)}, u32[]{:S(2)}, u32[]{:S(2)}) %collective-permute-start.6) | collective-permute-done | bytes 32800 | tf_op jit(solution)/shard_map/ppermute | solution.py:12
  64.9 1.1 collective-permute-done.7
  66.9 4.6 %all_gather.41 = f32[32,512]{1,0:T(8,128)S(1)} all-gather(f32[16,512]{1,0:T(8,128)S(1)} %broadcast_multiply_fusion.3), channel_id=1, replica_groups=mesh['region'=16,'tracer'=2] {'tracer'}, dimensions={0}, use_global_device_ids=true | all-gather | bytes 98304 | tf_op jit(solution)/shard_map/all_gather | solution.py:76
  71.7 0.5 multiply_reduce_fusion.18
  72.3 4.7 %collective-permute-start.8 = (f32[16,512]{1,0:T(8,128)S(1)}, f32[16,512]{1,0:T(8,128)S(1)}, u32[]{:S(2)}, u32[]{:S(2)}) collective-permute-start(f32[16,512]{1,0:T(8,128)S(1)} %get-tuple-element.20), channel_id=1, source_target_pairs={{4,0},{6,2},{8,4},{10,6},{12,8},{14,10},{16,12},{18,14},{20,16},{2... | collective-permute-start | bytes 98312 | tf_op jit(solution)/shard_map/ppermute | solution.py:12
  77.0 1.1 collective-permute-start.9
  78.4 0.6 collective-permute-done.11
  79.0 0.8 collective-permute-done.9
  80.7 4.6 %all_gather.43 = f32[32,512]{1,0:T(8,128)S(1)} all-gather(f32[16,512]{1,0:T(8,128)S(1)} %broadcast_multiply_fusion.2), channel_id=1, replica_groups=mesh['region'=16,'tracer'=2] {'tracer'}, dimensions={0}, use_global_device_ids=true | all-gather | bytes 98304 | tf_op jit(solution)/shard_map/all_gather | solution.py:76
  86.0 4.2 %collective-permute-start.12 = (f32[16,512]{1,0:T(8,128)S(1)}, f32[16,512]{1,0:T(8,128)S(1)}, u32[]{:S(2)}, u32[]{:S(2)}) collective-permute-start(f32[16,512]{1,0:T(8,128)S(1)} %get-tuple-element.15), channel_id=1, source_target_pairs={{4,0},{6,2},{8,4},{10,6},{12,8},{14,10},{16,12},{18,14},{20,16},{2... | collective-permute-start | bytes 98312 | tf_op jit(solution)/shard_map/ppermute | solution.py:12
  90.2 0.5 collective-permute-start.14
  90.7 1.0 collective-permute-start.15
  92.1 4.1 %collective-permute-done.14 = f32[16,512]{1,0:T(8,128)S(1)} collective-permute-done((f32[16,512]{1,0:T(8,128)S(1)}, f32[16,512]{1,0:T(8,128)S(1)}, u32[]{:S(2)}, u32[]{:S(2)}) %collective-permute-start.14) | collective-permute-done | bytes 32800 | tf_op jit(solution)/shard_map/ppermute | solution.py:12
  96.2 1.4 %collective-permute-done.15 = f32[16,512]{1,0:T(8,128)S(1)} collective-permute-done((f32[16,512]{1,0:T(8,128)S(1)}, f32[16,512]{1,0:T(8,128)S(1)}, u32[]{:S(2)}, u32[]{:S(2)}) %collective-permute-start.15) | collective-permute-done | bytes 32800 | tf_op jit(solution)/shard_map/ppermute | solution.py:12
  98.5 4.6 %all_gather.45 = f32[32,512]{1,0:T(8,128)S(1)} all-gather(f32[16,512]{1,0:T(8,128)S(1)} %broadcast_multiply_fusion.1), channel_id=1, replica_groups=mesh['region'=16,'tracer'=2] {'tracer'}, dimensions={0}, use_global_device_ids=true | all-gather | bytes 98304 | tf_op jit(solution)/shard_map/all_gather | solution.py:76
  103.9 0.5 collective-permute-start.18
  104.4 2.0 %collective-permute-start.19 = (f32[16,512]{1,0:T(8,128)S(1)}, f32[16,512]{1,0:T(8,128)S(1)}, u32[]{:S(2)}, u32[]{:S(2)}) collective-permute-start(f32[16,512]{1,0:T(8,128)S(1)} %get-tuple-element.11), channel_id=1, source_target_pairs={{28,0},{30,2},{0,4},{2,6},{4,8},{6,10},{8,12},{10,14},{12,16},{14,... | collective-permute-start | bytes 98312 | tf_op jit(solution)/shard_map/ppermute | solution.py:12
  106.6 1.1 collective-permute-done.16
  107.7 2.2 %collective-permute-done.18 = f32[16,512]{1,0:T(8,128)S(1)} collective-permute-done((f32[16,512]{1,0:T(8,128)S(1)}, f32[16,512]{1,0:T(8,128)S(1)}, u32[]{:S(2)}, u32[]{:S(2)}) %collective-permute-start.18) | collective-permute-done | bytes 32800 | tf_op jit(solution)/shard_map/ppermute | solution.py:12
  110.0 1.0 collective-permute-done.19
  111.9 4.6 %all_gather.47 = f32[32,512]{1,0:T(8,128)S(1)} all-gather(f32[16,512]{1,0:T(8,128)S(1)} %broadcast_multiply_fusion), channel_id=1, replica_groups=mesh['region'=16,'tracer'=2] {'tracer'}, dimensions={0}, use_global_device_ids=true | all-gather | bytes 98304 | tf_op jit(solution)/shard_map/all_gather | solution.py:76
  117.3 0.5 collective-permute-start.22
  117.8 2.0 %collective-permute-start.23 = (f32[16,512]{1,0:T(8,128)S(1)}, f32[16,512]{1,0:T(8,128)S(1)}, u32[]{:S(2)}, u32[]{:S(2)}) collective-permute-start(f32[16,512]{1,0:T(8,128)S(1)} %get-tuple-element.6), channel_id=1, source_target_pairs={{28,0},{30,2},{0,4},{2,6},{4,8},{6,10},{8,12},{10,14},{12,16},{14,... | collective-permute-start | bytes 98312 | tf_op jit(solution)/shard_map/ppermute | solution.py:12
  120.0 1.1 collective-permute-done.20
  121.1 2.2 %collective-permute-done.22 = f32[16,512]{1,0:T(8,128)S(1)} collective-permute-done((f32[16,512]{1,0:T(8,128)S(1)}, f32[16,512]{1,0:T(8,128)S(1)}, u32[]{:S(2)}, u32[]{:S(2)}) %collective-permute-start.22) | collective-permute-done | bytes 32800 | tf_op jit(solution)/shard_map/ppermute | solution.py:12
  123.4 1.0 collective-permute-done.23
  124.4 0.9 add_multiply_fusion
  (113 shorter events, 10.4 us)
Async XLA Ops:
  0.0 4.6 %copy-start = (bf16[1,5,512,512]{3,2,1,0:T(8,128)(2,1)S(1)}, bf16[1,5,512,512]{3,2,1,0:T(8,128)(2,1)}, u32[]{:S(2)}) copy-start(bf16[1,5,512,512]{3,2,1,0:T(8,128)(2,1)} %param.13) | copy-start | bytes 7864324
  0.0 17.8 %copy-start.4 = (f32[6,16,512]{2,1,0:T(8,128)S(1)}, f32[6,16,512]{2,1,0:T(8,128)}, u32[]{:S(2)}) copy-start(f32[6,16,512]{2,1,0:T(8,128)} %param.10) | copy-start | bytes 589828
  0.0 27.0 %copy-start.2 = (f32[32,32]{1,0:T(8,128)S(1)}, f32[32,32]{1,0:T(8,128)}, u32[]{:S(2)}) copy-start(f32[32,32]{1,0:T(8,128)} %param.16) | copy-start | bytes 12292
  0.8 11.4 %copy-start.5 = (f32[5]{0:T(128)}, f32[5]{0:T(128)S(1)}, u32[]{:S(2)}) copy-start(f32[5]{0:T(128)S(1)} %get-tuple-element.42) | copy-start | bytes 64
  0.8 46.2 %copy-start.7 = (f32[5]{0:T(128)}, f32[5]{0:T(128)S(1)}, u32[]{:S(2)}) copy-start(f32[5]{0:T(128)S(1)} %get-tuple-element.43) | copy-start | bytes 64
  0.8 46.2 %copy-start.9 = (f32[5]{0:T(128)}, f32[5]{0:T(128)S(1)}, u32[]{:S(2)}) copy-start(f32[5]{0:T(128)S(1)} %get-tuple-element.44) | copy-start | bytes 64
  0.8 46.2 %copy-start.11 = (f32[5]{0:T(128)}, f32[5]{0:T(128)S(1)}, u32[]{:S(2)}) copy-start(f32[5]{0:T(128)S(1)} %get-tuple-element.45) | copy-start | bytes 64
  3.8 42.7 %copy-start.3 = (f32[32,32]{1,0:T(8,128)S(1)}, f32[32,32]{1,0:T(8,128)}, u32[]{:S(2)}) copy-start(f32[32,32]{1,0:T(8,128)} %param.17) | copy-start | bytes 12292
  4.6 8.4 %copy-start.13 = (f32[5]{0:T(128)}, f32[5]{0:T(128)S(1)}, u32[]{:S(2)}) copy-start(f32[5]{0:T(128)S(1)} %compare_convert_fusion.4) | copy-start | bytes 64
  4.6 43.6 %copy-start.1 = (f32[16,32,32]{2,1,0:T(8,128)S(1)}, f32[16,32,32]{2,1,0:T(8,128)}, u32[]{:S(2)}) copy-start(f32[16,32,32]{2,1,0:T(8,128)} %param.11) | copy-start | bytes 196612
  5.7 41.2 %collective-permute-start = (f32[16,512]{1,0:T(8,128)}, f32[16,512]{1,0:T(8,128)}, u32[]{:S(2)}, u32[]{:S(2)}) collective-permute-start(f32[16,512]{1,0:T(8,128)} %get-tuple-element.30), channel_id=1, source_target_pairs={{4,0},{6,2},{8,4},{10,6},{12,8},{14,10},{16,12},{18,14},{20,16},{2... | collective-permute-start | bytes 98312 | tf_op jit(solution)/shard_map/ppermute | solution.py:12
  11.8 35.2 %collective-permute-start.1 = (f32[16,512]{1,0:T(8,128)}, f32[16,512]{1,0:T(8,128)}, u32[]{:S(2)}, u32[]{:S(2)}) collective-permute-start(f32[16,512]{1,0:T(8,128)} %get-tuple-element.33), channel_id=1, source_target_pairs={{2,0},{4,2},{6,4},{8,6},{10,8},{12,10},{14,12},{16,14},{18,16},{20... | collective-permute-start | bytes 98312 | tf_op jit(solution)/shard_map/ppermute | solution.py:12
  11.8 35.2 %collective-permute-start.2 = (f32[16,512]{1,0:T(8,128)}, f32[16,512]{1,0:T(8,128)}, u32[]{:S(2)}, u32[]{:S(2)}) collective-permute-start(f32[16,512]{1,0:T(8,128)} %get-tuple-element.32), channel_id=1, source_target_pairs={{30,0},{0,2},{2,4},{4,6},{6,8},{8,10},{10,12},{12,14},{14,16},{16,... | collective-permute-start | bytes 98312 | tf_op jit(solution)/shard_map/ppermute | solution.py:12
  12.3 34.7 %collective-permute-start.3 = (f32[16,512]{1,0:T(8,128)}, f32[16,512]{1,0:T(8,128)}, u32[]{:S(2)}, u32[]{:S(2)}) collective-permute-start(f32[16,512]{1,0:T(8,128)} %get-tuple-element.31), channel_id=1, source_target_pairs={{28,0},{30,2},{0,4},{2,6},{4,8},{6,10},{8,12},{10,14},{12,16},{14,... | collective-permute-start | bytes 98312 | tf_op jit(solution)/shard_map/ppermute | solution.py:12
  48.8 22.9 %copy-start.6 = (f32[5]{0:T(128)S(1)}, f32[5]{0:T(128)}, u32[]{:S(2)}) copy-start(f32[5]{0:T(128)} %copy-done.5) | copy-start | bytes 64
  48.8 22.9 %copy-start.8 = (f32[5]{0:T(128)S(1)}, f32[5]{0:T(128)}, u32[]{:S(2)}) copy-start(f32[5]{0:T(128)} %copy-done.7) | copy-start | bytes 64
  48.8 22.9 %copy-start.10 = (f32[5]{0:T(128)S(1)}, f32[5]{0:T(128)}, u32[]{:S(2)}) copy-start(f32[5]{0:T(128)} %copy-done.9) | copy-start | bytes 64
  48.8 22.9 %copy-start.12 = (f32[5]{0:T(128)S(1)}, f32[5]{0:T(128)}, u32[]{:S(2)}) copy-start(f32[5]{0:T(128)} %copy-done.11) | copy-start | bytes 64
  48.8 22.9 %copy-start.14 = (f32[5]{0:T(128)S(1)}, f32[5]{0:T(128)}, u32[]{:S(2)}) copy-start(f32[5]{0:T(128)} %copy-done.13) | copy-start | bytes 64
  54.8 5.7 %collective-permute-start.4 = (f32[16,512]{1,0:T(8,128)S(1)}, f32[16,512]{1,0:T(8,128)S(1)}, u32[]{:S(2)}, u32[]{:S(2)}) collective-permute-start(f32[16,512]{1,0:T(8,128)S(1)} %get-tuple-element.25), channel_id=1, source_target_pairs={{4,0},{6,2},{8,4},{10,6},{12,8},{14,10},{16,12},{18,14},{20,16},{2... | collective-permute-start | bytes 98312 | tf_op jit(solution)/shard_map/ppermute | solution.py:12
  58.9 1.9 %collective-permute-start.5 = (f32[16,512]{1,0:T(8,128)S(1)}, f32[16,512]{1,0:T(8,128)S(1)}, u32[]{:S(2)}, u32[]{:S(2)}) collective-permute-start(f32[16,512]{1,0:T(8,128)S(1)} %get-tuple-element.28), channel_id=1, source_target_pairs={{2,0},{4,2},{6,4},{8,6},{10,8},{12,10},{14,12},{16,14},{18,16},{20... | collective-permute-start | bytes 98312 | tf_op jit(solution)/shard_map/ppermute | solution.py:12
  58.9 6.0 %collective-permute-start.6 = (f32[16,512]{1,0:T(8,128)S(1)}, f32[16,512]{1,0:T(8,128)S(1)}, u32[]{:S(2)}, u32[]{:S(2)}) collective-permute-start(f32[16,512]{1,0:T(8,128)S(1)} %get-tuple-element.27), channel_id=1, source_target_pairs={{30,0},{0,2},{2,4},{4,6},{6,8},{8,10},{10,12},{12,14},{14,16},{16,... | collective-permute-start | bytes 98312 | tf_op jit(solution)/shard_map/ppermute | solution.py:12
  59.4 6.6 %collective-permute-start.7 = (f32[16,512]{1,0:T(8,128)S(1)}, f32[16,512]{1,0:T(8,128)S(1)}, u32[]{:S(2)}, u32[]{:S(2)}) collective-permute-start(f32[16,512]{1,0:T(8,128)S(1)} %get-tuple-element.26), channel_id=1, source_target_pairs={{28,0},{30,2},{0,4},{2,6},{4,8},{6,10},{8,12},{10,14},{12,16},{14,... | collective-permute-start | bytes 98312 | tf_op jit(solution)/shard_map/ppermute | solution.py:12
  72.2 6.2 %collective-permute-start.10 = (f32[16,512]{1,0:T(8,128)S(1)}, f32[16,512]{1,0:T(8,128)S(1)}, u32[]{:S(2)}, u32[]{:S(2)}) collective-permute-start(f32[16,512]{1,0:T(8,128)S(1)} %get-tuple-element.22), channel_id=1, source_target_pairs={{30,0},{0,2},{2,4},{4,6},{6,8},{8,10},{10,12},{12,14},{14,16},{16,... | collective-permute-start | bytes 98312 | tf_op jit(solution)/shard_map/ppermute | solution.py:12
  72.3 6.7 %collective-permute-start.11 = (f32[16,512]{1,0:T(8,128)S(1)}, f32[16,512]{1,0:T(8,128)S(1)}, u32[]{:S(2)}, u32[]{:S(2)}) collective-permute-start(f32[16,512]{1,0:T(8,128)S(1)} %get-tuple-element.21), channel_id=1, source_target_pairs={{28,0},{30,2},{0,4},{2,6},{4,8},{6,10},{8,12},{10,14},{12,16},{14,... | collective-permute-start | bytes 98312 | tf_op jit(solution)/shard_map/ppermute | solution.py:12
  72.3 6.7 %collective-permute-start.8 = (f32[16,512]{1,0:T(8,128)S(1)}, f32[16,512]{1,0:T(8,128)S(1)}, u32[]{:S(2)}, u32[]{:S(2)}) collective-permute-start(f32[16,512]{1,0:T(8,128)S(1)} %get-tuple-element.20), channel_id=1, source_target_pairs={{4,0},{6,2},{8,4},{10,6},{12,8},{14,10},{16,12},{18,14},{20,16},{2... | collective-permute-start | bytes 98312 | tf_op jit(solution)/shard_map/ppermute | solution.py:12
  77.0 2.7 %collective-permute-start.9 = (f32[16,512]{1,0:T(8,128)S(1)}, f32[16,512]{1,0:T(8,128)S(1)}, u32[]{:S(2)}, u32[]{:S(2)}) collective-permute-start(f32[16,512]{1,0:T(8,128)S(1)} %get-tuple-element.23), channel_id=1, source_target_pairs={{2,0},{4,2},{6,4},{8,6},{10,8},{12,10},{14,12},{16,14},{18,16},{20... | collective-permute-start | bytes 98312 | tf_op jit(solution)/shard_map/ppermute | solution.py:12
  86.0 6.0 %collective-permute-start.12 = (f32[16,512]{1,0:T(8,128)S(1)}, f32[16,512]{1,0:T(8,128)S(1)}, u32[]{:S(2)}, u32[]{:S(2)}) collective-permute-start(f32[16,512]{1,0:T(8,128)S(1)} %get-tuple-element.15), channel_id=1, source_target_pairs={{4,0},{6,2},{8,4},{10,6},{12,8},{14,10},{16,12},{18,14},{20,16},{2... | collective-permute-start | bytes 98312 | tf_op jit(solution)/shard_map/ppermute | solution.py:12
  90.2 1.9 %collective-permute-start.13 = (f32[16,512]{1,0:T(8,128)S(1)}, f32[16,512]{1,0:T(8,128)S(1)}, u32[]{:S(2)}, u32[]{:S(2)}) collective-permute-start(f32[16,512]{1,0:T(8,128)S(1)} %get-tuple-element.18), channel_id=1, source_target_pairs={{2,0},{4,2},{6,4},{8,6},{10,8},{12,10},{14,12},{16,14},{18,16},{20... | collective-permute-start | bytes 98312 | tf_op jit(solution)/shard_map/ppermute | solution.py:12
  90.2 6.0 %collective-permute-start.14 = (f32[16,512]{1,0:T(8,128)S(1)}, f32[16,512]{1,0:T(8,128)S(1)}, u32[]{:S(2)}, u32[]{:S(2)}) collective-permute-start(f32[16,512]{1,0:T(8,128)S(1)} %get-tuple-element.17), channel_id=1, source_target_pairs={{30,0},{0,2},{2,4},{4,6},{6,8},{8,10},{10,12},{12,14},{14,16},{16,... | collective-permute-start | bytes 98312 | tf_op jit(solution)/shard_map/ppermute | solution.py:12
  90.7 6.9 %collective-permute-start.15 = (f32[16,512]{1,0:T(8,128)S(1)}, f32[16,512]{1,0:T(8,128)S(1)}, u32[]{:S(2)}, u32[]{:S(2)}) collective-permute-start(f32[16,512]{1,0:T(8,128)S(1)} %get-tuple-element.16), channel_id=1, source_target_pairs={{28,0},{30,2},{0,4},{2,6},{4,8},{6,10},{8,12},{10,14},{12,16},{14,... | collective-permute-start | bytes 98312 | tf_op jit(solution)/shard_map/ppermute | solution.py:12
  103.8 4.0 %collective-permute-start.16 = (f32[16,512]{1,0:T(8,128)S(1)}, f32[16,512]{1,0:T(8,128)S(1)}, u32[]{:S(2)}, u32[]{:S(2)}) collective-permute-start(f32[16,512]{1,0:T(8,128)S(1)} %get-tuple-element.10), channel_id=1, source_target_pairs={{4,0},{6,2},{8,4},{10,6},{12,8},{14,10},{16,12},{18,14},{20,16},{2... | collective-permute-start | bytes 98312 | tf_op jit(solution)/shard_map/ppermute | solution.py:12
  103.8 3.9 %collective-permute-start.17 = (f32[16,512]{1,0:T(8,128)S(1)}, f32[16,512]{1,0:T(8,128)S(1)}, u32[]{:S(2)}, u32[]{:S(2)}) collective-permute-start(f32[16,512]{1,0:T(8,128)S(1)} %get-tuple-element.13), channel_id=1, source_target_pairs={{2,0},{4,2},{6,4},{8,6},{10,8},{12,10},{14,12},{16,14},{18,16},{20... | collective-permute-start | bytes 98312 | tf_op jit(solution)/shard_map/ppermute | solution.py:12
  103.9 6.1 %collective-permute-start.18 = (f32[16,512]{1,0:T(8,128)S(1)}, f32[16,512]{1,0:T(8,128)S(1)}, u32[]{:S(2)}, u32[]{:S(2)}) collective-permute-start(f32[16,512]{1,0:T(8,128)S(1)} %get-tuple-element.12), channel_id=1, source_target_pairs={{30,0},{0,2},{2,4},{4,6},{6,8},{8,10},{10,12},{12,14},{14,16},{16,... | collective-permute-start | bytes 98312 | tf_op jit(solution)/shard_map/ppermute | solution.py:12
  104.4 6.6 %collective-permute-start.19 = (f32[16,512]{1,0:T(8,128)S(1)}, f32[16,512]{1,0:T(8,128)S(1)}, u32[]{:S(2)}, u32[]{:S(2)}) collective-permute-start(f32[16,512]{1,0:T(8,128)S(1)} %get-tuple-element.11), channel_id=1, source_target_pairs={{28,0},{30,2},{0,4},{2,6},{4,8},{6,10},{8,12},{10,14},{12,16},{14,... | collective-permute-start | bytes 98312 | tf_op jit(solution)/shard_map/ppermute | solution.py:12
  117.2 4.0 %collective-permute-start.20 = (f32[16,512]{1,0:T(8,128)S(1)}, f32[16,512]{1,0:T(8,128)S(1)}, u32[]{:S(2)}, u32[]{:S(2)}) collective-permute-start(f32[16,512]{1,0:T(8,128)S(1)} %get-tuple-element.5), channel_id=1, source_target_pairs={{4,0},{6,2},{8,4},{10,6},{12,8},{14,10},{16,12},{18,14},{20,16},{2... | collective-permute-start | bytes 98312 | tf_op jit(solution)/shard_map/ppermute | solution.py:12
  117.2 3.9 %collective-permute-start.21 = (f32[16,512]{1,0:T(8,128)S(1)}, f32[16,512]{1,0:T(8,128)S(1)}, u32[]{:S(2)}, u32[]{:S(2)}) collective-permute-start(f32[16,512]{1,0:T(8,128)S(1)} %get-tuple-element.8), channel_id=1, source_target_pairs={{2,0},{4,2},{6,4},{8,6},{10,8},{12,10},{14,12},{16,14},{18,16},{20... | collective-permute-start | bytes 98312 | tf_op jit(solution)/shard_map/ppermute | solution.py:12
  117.3 6.1 %collective-permute-start.22 = (f32[16,512]{1,0:T(8,128)S(1)}, f32[16,512]{1,0:T(8,128)S(1)}, u32[]{:S(2)}, u32[]{:S(2)}) collective-permute-start(f32[16,512]{1,0:T(8,128)S(1)} %get-tuple-element.7), channel_id=1, source_target_pairs={{30,0},{0,2},{2,4},{4,6},{6,8},{8,10},{10,12},{12,14},{14,16},{16,... | collective-permute-start | bytes 98312 | tf_op jit(solution)/shard_map/ppermute | solution.py:12
  117.8 6.6 %collective-permute-start.23 = (f32[16,512]{1,0:T(8,128)S(1)}, f32[16,512]{1,0:T(8,128)S(1)}, u32[]{:S(2)}, u32[]{:S(2)}) collective-permute-start(f32[16,512]{1,0:T(8,128)S(1)} %get-tuple-element.6), channel_id=1, source_target_pairs={{28,0},{30,2},{0,4},{2,6},{4,8},{6,10},{8,12},{10,14},{12,16},{14,... | collective-permute-start | bytes 98312 | tf_op jit(solution)/shard_map/ppermute | solution.py:12
where the time goes:
time: 126 us; the launch traced here: 125 us
  blocking collectives  55.2 us (44%)
  starting transfers between devices  28.6 us (23%)
  waiting for transfers between devices  22.2 us (18%)
  matrix products  13.3 us (11%)
  local copies, waits for them, and re-layouts  3.16 us (3%)
  other arithmetic  1.63 us (1%)
  between operations  1.29 us (1%)
    ppermute x24, starting transfers between devices, from_behind(): return lax.ppermute(block, axis, route)  28.6 us
    all_gather x6, blocking collectives, local(): lax.all_gather(state, 'tracer', axis=0, tiled=True)  27.6 us
    all_gather x6, blocking collectives, local(): lax.all_gather(settled, 'tracer', axis=0, tiled=True)  27.6 us
    ppermute x24, waiting for transfers between devices, from_behind(): return lax.ppermute(block, axis, route)  22.2 us
    dot_general x6, matrix products, local(): jnp.einsum('tb,kbc->ktc', settled_half, tile_block, preferred_element_typ...  4.17 us
    dot_general x6, matrix products, local(): reacted = jnp.dot(own_rows.T, weighted, precision=highest)  3.22 us
    dot_general x6, matrix products, local(): jnp.einsum('tcm,cml->tcl', adjoint.reshape(tr_dev, columns, levels), impl...  3.18 us
  transfers between devices with their start and end apart: 24, of which 15 were waited for; matrix products, arithmetic and copies ran while one was open for 2% of the time, Pallas kernels for 0%

commit v1 on v0

v1 whole, which is shorter than its diff:
```python
import functools

import jax
import jax.numpy as jnp
from jax import lax
from jax.experimental import pallas as pl
from jax.experimental.pallas import tpu as pltpu
from jax.sharding import PartitionSpec as P

MESH = pl.DeviceIdType.MESH
F32, BF16 = jnp.float32, jnp.bfloat16
LANES = 128
ROWS_DIM = (((1,), (1,)), ((), ()))


def halves(x):
    high = x.astype(BF16)
    return high, (x - high.astype(F32)).astype(BF16)


def dot(a, b):
    return jnp.dot(a, b, preferred_element_type=F32)


def dot_split(a, b):
    (a_high, a_low), (b_high, b_low) = a, halves(b)
    return dot(a_high, b_high) + (dot(a_high, b_low) + dot(a_low, b_high))


def kernel(
    cot_hbm, states_hbm, inv_hbm, wet, tiles_hbm, off, cnt, up_hbm, rel_hbm,
    out,
    tiles, inv, up, rel, adj, full_state, full_settled, gain,
    relay_out, direct_out, peer_out, merged_out,
    relay_in, direct_in, peer_in, merged_in,
    load_sem, own_sem, send_sem, recv_sem, settled_send, settled_recv, state_send, state_recv,
):
    steps, tracers_n, tr, boxes = full_state.shape
    columns, levels, _ = inv.shape
    slots = tiles.shape[0]
    ntr = tracers_n * tr
    region, tracer = lax.axis_index("region"), lax.axis_index("tracer")
    regions = lax.axis_size("region")

    sign = 2 * lax.rem(region, 2) - 1
    at = lambda distance: lax.rem(region + distance * sign + 2 * regions, regions)
    inner, outer, far, behind = at(-1), at(1), at(2), at(-2)
    others = [lax.rem(tracer + j, tracers_n) for j in range(1, tracers_n)]

    loads = [
        pltpu.make_async_copy(src, dst, load_sem.at[k])
        for k, (src, dst) in enumerate(
            [(inv_hbm, inv), (cot_hbm, adj), (up_hbm, up), (rel_hbm, rel), (tiles_hbm.at[0], tiles)]
        )
    ]
    for load in loads:
        load.start()
    own_states = [
        pltpu.make_async_copy(states_hbm.at[n], full_state.at[n, tracer], own_sem.at[n])
        for n in range(steps)
    ]
    for copy in own_states[::-1]:
        copy.start()

    barrier = pltpu.get_barrier_semaphore()
    for device in (inner, outer, behind):
        pl.semaphore_signal(barrier, inc=1, device_id={"region": device}, device_id_type=MESH)
    for other in others:
        pl.semaphore_signal(barrier, inc=1, device_id={"tracer": other}, device_id_type=MESH)
    pl.semaphore_wait(barrier, 3 + len(others))

    def state_copy(n, j):
        return pltpu.make_async_remote_copy(
            src_ref=states_hbm.at[n],
            dst_ref=full_state.at[n, tracer],
            send_sem=state_send.at[n, j],
            recv_sem=state_recv.at[n, j],
            device_id={"tracer": others[j]},
            device_id_type=MESH,
        )

    def settled_copy(i, j):
        return pltpu.make_async_remote_copy(
            src_ref=full_settled.at[i, tracer],
            dst_ref=full_settled.at[i, tracer],
            send_sem=settled_send.at[i, j],
            recv_sem=settled_recv.at[i, j],
            device_id={"tracer": others[j]},
            device_id_type=MESH,
        )

    def region_copy(i, k):
        src, dst, target = (
            (relay_out, relay_in, inner),
            (direct_out, direct_in, far),
            (peer_out, peer_in, inner),
            (merged_out, merged_in, outer),
        )[k]
        return pltpu.make_async_remote_copy(
            src_ref=src.at[i],
            dst_ref=dst.at[i],
            send_sem=send_sem.at[i, k],
            recv_sem=recv_sem.at[i, k],
            device_id={"region": target},
            device_id_type=MESH,
        )

    peers = range(len(others))
    for n in range(steps - 1, max(steps - 3, -1), -1):
        for j in peers:
            state_copy(n, j).start()

    lane = lax.broadcasted_iota(jnp.int32, (1, boxes), 1)
    wet_of = jnp.zeros((1, boxes), jnp.int32)
    for c in range(columns):
        wet_of = jnp.where(lane // levels == c, wet[c], wet_of)
    wet_mask = (lane % levels < wet_of).astype(F32)

    def tile_at(distance):
        slot, live = jnp.int32(0), jnp.int32(0)
        for k in range(slots):
            hit = jnp.logical_and(off[0, k] == distance * sign, k < cnt[0])
            slot = jnp.where(hit, k, slot)
            live = jnp.where(hit, 1, live)
        return slot, live.astype(F32)

    places = {d: tile_at(d) for d in (-2, 2, -1, 1, 0)}

    for load in loads[:4]:
        load.wait()
    per = LANES // levels
    flat = inv[...].reshape(boxes, levels)
    wide = jnp.concatenate([flat] * per, axis=1)
    row = lax.broadcasted_iota(jnp.int32, (boxes, LANES), 0)
    lanes = lax.broadcasted_iota(jnp.int32, (boxes, LANES), 1)
    wide = jnp.where((row // levels) % per == lanes // levels, wide, 0.0)
    blocks = []
    for b in range(boxes // LANES):
        span = slice(b * LANES, (b + 1) * LANES)
        high, low = halves(wide[span] * wet_mask[:, span])
        blocks.append(jnp.concatenate([high, low], axis=0))

    ident = (
        lax.broadcasted_iota(jnp.int32, (ntr, ntr), 0) == lax.broadcasted_iota(jnp.int32, (ntr, ntr), 1)
    ).astype(F32)
    own_rows = (
        lax.broadcasted_iota(jnp.int32, (tr, ntr), 0) + tracer * tr
        == lax.broadcasted_iota(jnp.int32, (tr, ntr), 1)
    ).astype(F32)
    highest = lax.Precision.HIGHEST
    uptake = halves(up[...])
    uptake_own = halves(
        lax.dot_general(own_rows, up[...], ROWS_DIM, precision=highest, preferred_element_type=F32)
    )
    release = halves(
        lax.dot_general(ident, rel[...], ROWS_DIM, precision=highest, preferred_element_type=F32)
    )

    def joined(ref, i):
        if tr % 8 == 0:
            return ref[i].reshape(ntr, boxes)
        return jnp.concatenate([ref[i, j] for j in range(tracers_n)], axis=0)

    def settle(a):
        high, low = halves(a)
        zero = jnp.zeros((tr, LANES), BF16)
        parts = []
        for b, block in enumerate(blocks):
            span = slice(b * LANES, (b + 1) * LANES)
            first = jnp.concatenate([high[:, span], high[:, span]], axis=1)
            second = jnp.concatenate([low[:, span], zero], axis=1)
            if tr % 16 == 0:
                both = dot(jnp.concatenate([first, second], axis=0), block)
                parts.append(both[:tr] + both[tr:])
            else:
                parts.append(dot(first, block) + dot(second, block))
        return jnp.concatenate(parts, axis=1)

    def make_gain(n):
        for j in peers:
            state_copy(n, j).wait_recv()
        pltpu.make_async_copy(states_hbm.at[n], full_state.at[n, tracer], own_sem.at[n]).wait()
        bent = jnp.tanh(dot_split(uptake, joined(full_state, n)))
        gain[...] = 1.0 - bent * bent

    def step(i, carry):
        n = steps - 1 - i
        settled = settle(adj[...])
        full_settled[i, tracer] = settled
        for j in peers:
            settled_copy(i, j).start()
        half = settled.astype(BF16)

        @pl.when(i == 0)
        def _():
            loads[4].wait()

        def term(distance):
            slot, live = places[distance]
            return dot(half, tiles[slot]) * live

        relay_out[i] = term(-2)
        region_copy(i, 0).start()
        direct_out[i] = term(2)
        region_copy(i, 1).start()
        near = term(1)
        region_copy(i, 0).wait_recv()
        merged_out[i] = near + relay_in[i]
        region_copy(i, 3).start()
        peer_out[i] = term(-1)
        region_copy(i, 2).start()

        @pl.when(n >= 2)
        def _():
            for j in peers:
                state_copy(n - 2, j).start()

        total = term(0)

        @pl.when(i == 0)
        def _():
            make_gain(n)

        for j in peers:
            settled_copy(i, j).wait_recv()
        weighted = gain[...] * dot_split(release, joined(full_settled, i))
        total = total + dot_split(uptake_own, weighted)

        @pl.when(n >= 1)
        def _():
            make_gain(n - 1)

        region_copy(i, 2).wait_recv()
        total = total + peer_in[i]
        region_copy(i, 1).wait_recv()
        total = total + direct_in[i]
        region_copy(i, 3).wait_recv()
        adj[...] = wet_mask * (total + merged_in[i])
        return carry

    lax.fori_loop(0, steps, step, 0)
    out[...] = adj[...]

    def drain(i, carry):
        for k in range(4):
            region_copy(i, k).wait_send()
        for j in peers:
            settled_copy(i, j).wait_send()
            state_copy(i, j).wait_send()
        return carry

    lax.fori_loop(0, steps, drain, 0)


def local(
    cotangent,
    states,
    implicit_inverse,
    wet_levels,
    explicit_tiles,
    tile_offset,
    tile_count,
    uptake_weight,
    release_weight,
):
    tr, boxes = cotangent.shape
    steps = states.shape[0]
    tracers_n = lax.axis_size("tracer")
    ntr = tracers_n * tr
    slots = explicit_tiles.shape[1]
    peers = max(tracers_n - 1, 1)
    hbm = pl.BlockSpec(memory_space=pl.ANY)
    smem = pl.BlockSpec(memory_space=pltpu.SMEM)
    message = pltpu.VMEM((steps, tr, boxes), F32)
    gathered = pltpu.VMEM((steps, tracers_n, tr, boxes), F32)
    sems = pltpu.SemaphoreType.DMA
    return pl.pallas_call(
        kernel,
        out_shape=jax.ShapeDtypeStruct((tr, boxes), F32),
        in_specs=[hbm, hbm, hbm, smem, hbm, smem, smem, hbm, hbm],
        out_specs=pl.BlockSpec(memory_space=pltpu.VMEM),
        scratch_shapes=[
            pltpu.VMEM(explicit_tiles.shape[1:], BF16),
            pltpu.VMEM(implicit_inverse.shape, F32),
            pltpu.VMEM(uptake_weight.shape, F32),
            pltpu.VMEM(release_weight.shape, F32),
            pltpu.VMEM((tr, boxes), F32),
            gathered,
            gathered,
            pltpu.VMEM((ntr, boxes), F32),
        ]
        + [message] * 8
        + [
            sems((5,)),
            sems((steps,)),
            sems((steps, 4)),
            sems((steps, 4)),
            sems((steps, peers)),
            sems((steps, peers)),
            sems((steps, peers)),
            sems((steps, peers)),
        ],
        compiler_params=pltpu.CompilerParams(
            collective_id=0, has_side_effects=True, vmem_limit_bytes=40 * 1024 * 1024
        ),
        name="adjoint_steps",
    )(
        cotangent,
        states,
        implicit_inverse,
        wet_levels,
        explicit_tiles,
        tile_offset,
        tile_count,
        uptake_weight,
        release_weight,
    )


def solution(mesh):
    placed = (
        P("tracer", "region"),
        P(None, "tracer", "region"),
        P("region", None, None),
        P("region"),
        P("region", None, None, None),
        P("region", None),
        P("region"),
        P(),
        P(),
    )
    return jax.shard_map(
        local, mesh=mesh, in_specs=placed, out_specs=P("tracer", "region"), check_vma=False
    )
```

time: 126 us -> 46.9 us (0.37)
  blocking collectives: 55.2 us -> 0 us
  Pallas kernels: 0 us -> 38.1 us
  starting transfers between devices: 28.6 us -> 0 us
  waiting for transfers between devices: 22.2 us -> 0 us
  matrix products: 13.3 us -> 0 us
  local copies, waits for them, and re-layouts: 3.16 us -> 7.73 us
  other arithmetic: 1.63 us -> 0 us
    all_gather x12 -> x0, blocking collectives: 55.2 us -> none  [the longest x6 27.6 us: local(): lax.all_gather(state, 'tracer', axis=0, tiled=True)]
    pallas_call x0 -> x1, Pallas kernels: none -> 38.1 us  [local(): pl.pallas_call(kernel, out_shape=jax.ShapeDtypeStruct((tr, boxes), F32),...]
    ppermute x24 -> x0, starting transfers between devices: 28.6 us -> none  [from_behind(): return lax.ppermute(block, axis, route)]
    ppermute x24 -> x0, waiting for transfers between devices: 22.2 us -> none  [from_behind(): return lax.ppermute(block, axis, route)]
    dot_general x30 -> x0, matrix products: 13.3 us -> none  [the longest x6 4.17 us: local(): jnp.einsum('tb,kbc->ktc', settled_half, tile_block, preferred_element_typ...]
    unnamed x30 -> x17, local copies, waits for them, and re-layouts: 0.06 us -> 7.73 us
    reshape x12 -> x0, local copies, waits for them, and re-layouts: 1.92 us -> none  [the longest x6 1.29 us: local(): adjoint.reshape(tr_dev, columns, levels)]
    convert_element_type x3 -> x0, other arithmetic: 1.59 us -> none  [the longest x1 0.81 us: at_distance(): select = (offsets == distance).astype(jnp.float32)]
  transfers between devices with their start and end apart: 24 -> 0, of which waited for: 15 -> 0; matrix products, arithmetic and copies ran while one was open for 2% -> 0% of each run, Pallas kernels for 0% -> 0%
where the time goes in v1:
time: 46.9 us; the launch traced here: 46.5 us
  Pallas kernels  38.1 us (81%)
  local copies, waits for them, and re-layouts  7.73 us (16%)
  between operations  0.68 us (1%)
    pallas_call x1, Pallas kernels, local(): pl.pallas_call(kernel, out_shape=jax.ShapeDtypeStruct((tr, boxes), F32),...  38.1 us
    unnamed x17, local copies, waits for them, and re-layouts  7.73 us

profile of v1, /device:TPU:0, one launch (start us, length us, event | category | flops | bytes accessed | tf_op | source)
XLA Modules:
  0.0 46.5 jit_solution(5145070382694595265)
XLA Ops:
  0.7 0.0 copy-start
  0.7 1.7 %copy-done = bf16[1,5,512,512]{3,2,1,0:T(8,128)(2,1)S(1)} copy-done((bf16[1,5,512,512]{3,2,1,0:T(8,128)(2,1)S(1)}, bf16[1,5,512,512]{3,2,1,0:T(8,128)(2,1)}, u32[]{:S(2)}) %copy-start) | copy-done | bytes 2621464
  2.4 0.0 copy-start.1
  2.4 0.9 %copy-done.1 = f32[16,32,32]{2,1,0:T(8,128)S(1)} copy-done((f32[16,32,32]{2,1,0:T(8,128)S(1)}, f32[16,32,32]{2,1,0:T(8,128)}, u32[]{:S(2)}) %copy-start.1) | copy-done | bytes 65560
  3.3 0.0 copy-start.2
  3.3 0.9 %copy-done.2 = f32[6,16,512]{2,1,0:T(8,128)S(1)} copy-done((f32[6,16,512]{2,1,0:T(8,128)S(1)}, f32[6,16,512]{2,1,0:T(8,128)}, u32[]{:S(2)}) %copy-start.2) | copy-done | bytes 196632
  4.3 0.0 copy-start.3
  4.3 0.8 %copy-done.3 = f32[16,512]{1,0:T(8,128)S(1)} copy-done((f32[16,512]{1,0:T(8,128)S(1)}, f32[16,512]{1,0:T(8,128)}, u32[]{:S(2)}) %copy-start.3) | copy-done | bytes 32792
  5.0 0.0 copy-start.4
  5.0 0.7 %copy-done.4 = f32[32,32]{1,0:T(8,128)S(1)} copy-done((f32[32,32]{1,0:T(8,128)S(1)}, f32[32,32]{1,0:T(8,128)}, u32[]{:S(2)}) %copy-start.4) | copy-done | bytes 4120
  5.7 0.0 copy-start.5
  5.7 0.7 %copy-done.5 = f32[32,32]{1,0:T(8,128)S(1)} copy-done((f32[32,32]{1,0:T(8,128)S(1)}, f32[32,32]{1,0:T(8,128)}, u32[]{:S(2)}) %copy-start.5) | copy-done | bytes 4120
  6.5 0.0 copy-start.6
  6.5 0.7 %copy-done.6 = s32[16]{0:T(128)S(1)} copy-done((s32[16]{0:T(128)S(1)}, s32[16]{0:T(128)}, u32[]{:S(2)}) %copy-start.6) | copy-done | bytes 88
  7.1 0.0 copy-start.7
  7.1 0.7 %copy-done.7 = s32[1,5]{1,0:T(1,128)S(1)} copy-done((s32[1,5]{1,0:T(1,128)S(1)}, s32[1,5]{1,0:T(1,128)}, u32[]{:S(2)}) %copy-start.7) | copy-done | bytes 44
  7.8 38.1 %adjoint_steps.1 = f32[16,512]{1,0:T(8,128)S(1)} custom-call(f32[16,512]{1,0:T(8,128)S(1)} %copy-done.3, f32[6,16,512]{2,1,0:T(8,128)S(1)} %copy-done.2, f32[16,32,32]{2,1,0:T(8,128)S(1)} %copy-done.1, s32[16]{0:T(128)S(1)} %copy-done.6, bf16[1,5,512,512]{3,2,1,0:T(8,128)(2,1)S(1)} %copy-done, s32[1,5]{1,0:T(1,128)S(1)} %copy-done.7, s32[1]{0:T(128)S(6)} %copy.11.cnt, ...), custom_call_target="tpu_custom_call" | custom-call | tf_op jit(solution)/shard_map/adjoint_steps/pallas_call | solution.py:277
  45.8 0.6 %copy.12 = f32[16,512]{1,0:T(8,128)} copy(f32[16,512]{1,0:T(8,128)S(1)} %adjoint_steps.1) | data formatting | bytes 65536
Async XLA Ops:
  0.7 1.7 %copy-start = (bf16[1,5,512,512]{3,2,1,0:T(8,128)(2,1)S(1)}, bf16[1,5,512,512]{3,2,1,0:T(8,128)(2,1)}, u32[]{:S(2)}) copy-start(bf16[1,5,512,512]{3,2,1,0:T(8,128)(2,1)} %tiles_hbm.1) | copy-start | bytes 7864324
  2.4 0.9 %copy-start.1 = (f32[16,32,32]{2,1,0:T(8,128)S(1)}, f32[16,32,32]{2,1,0:T(8,128)}, u32[]{:S(2)}) copy-start(f32[16,32,32]{2,1,0:T(8,128)} %inv_hbm.1) | copy-start | bytes 196612
  3.3 0.9 %copy-start.2 = (f32[6,16,512]{2,1,0:T(8,128)S(1)}, f32[6,16,512]{2,1,0:T(8,128)}, u32[]{:S(2)}) copy-start(f32[6,16,512]{2,1,0:T(8,128)} %states_hbm.1) | copy-start | bytes 589828
  4.3 0.8 %copy-start.3 = (f32[16,512]{1,0:T(8,128)S(1)}, f32[16,512]{1,0:T(8,128)}, u32[]{:S(2)}) copy-start(f32[16,512]{1,0:T(8,128)} %cot_hbm.1) | copy-start | bytes 98308
  5.0 0.7 %copy-start.4 = (f32[32,32]{1,0:T(8,128)S(1)}, f32[32,32]{1,0:T(8,128)}, u32[]{:S(2)}) copy-start(f32[32,32]{1,0:T(8,128)} %up_hbm.1) | copy-start | bytes 12292
  5.7 0.7 %copy-start.5 = (f32[32,32]{1,0:T(8,128)S(1)}, f32[32,32]{1,0:T(8,128)}, u32[]{:S(2)}) copy-start(f32[32,32]{1,0:T(8,128)} %rel_hbm.1) | copy-start | bytes 12292
  6.5 0.7 %copy-start.6 = (s32[16]{0:T(128)S(1)}, s32[16]{0:T(128)}, u32[]{:S(2)}) copy-start(s32[16]{0:T(128)} %wet.1) | copy-start | bytes 196
  7.1 0.7 %copy-start.7 = (s32[1,5]{1,0:T(1,128)S(1)}, s32[1,5]{1,0:T(1,128)}, u32[]{:S(2)}) copy-start(s32[1,5]{1,0:T(1,128)} %off.1) | copy-start | bytes 64

commit v2 on v1

--- a/solution.py
+++ b/solution.py
@@ -301,7 +301,7 @@
             sems((steps, peers)),
         ],
         compiler_params=pltpu.CompilerParams(
-            collective_id=0, has_side_effects=True, vmem_limit_bytes=40 * 1024 * 1024
+            collective_id=0, has_side_effects=True, vmem_limit_bytes=60 * 1024 * 1024
         ),
         name="adjoint_steps",
     )(

time: 46.9 us -> 40.5 us (0.86)
  local copies, waits for them, and re-layouts: 7.73 us -> 1.38 us
    unnamed x17 -> x1, local copies, waits for them, and re-layouts: 7.73 us -> 1.38 us
where the time goes in v2:
time: 40.5 us; the launch traced here: 40.3 us
  Pallas kernels  38.3 us (95%)
  local copies, waits for them, and re-layouts  1.38 us (3%)
  between operations  0.66 us (2%)
    pallas_call x1, Pallas kernels, local(): pl.pallas_call(kernel, out_shape=jax.ShapeDtypeStruct((tr, boxes), F32),...  38.3 us
    unnamed x1, local copies, waits for them, and re-layouts  1.38 us

profile of v2, /device:TPU:0, one launch (start us, length us, event | category | flops | bytes accessed | tf_op | source)
XLA Modules:
  0.0 40.3 jit_solution(7364182828730540224)
XLA Ops:
  0.7 38.3 %adjoint_steps.1 = f32[16,512]{1,0:T(8,128)} custom-call(f32[16,512]{1,0:T(8,128)} %cot_hbm.1, f32[6,16,512]{2,1,0:T(8,128)} %states_hbm.1, f32[16,32,32]{2,1,0:T(8,128)} %inv_hbm.1, s32[16]{0:T(128)} %wet.1, bf16[1,5,512,512]{3,2,1,0:T(8,128)(2,1)} %tiles_hbm.1, s32[1,5]{1,0:T(1,128)} %off.1, s32[1]{0:T(128)S(6)} %copy.11.cnt, f32[32,32]{1,0:T(8,128)} %up_hbm.1, ...), custom_call_target="tpu_custom_call" | custom-call | tf_op jit(solution)/shard_map/adjoint_steps/pallas_call | solution.py:277
  39.0 1.4 %copy.12 = f32[16,512]{1,0:T(8,128)} copy(f32[16,512]{1,0:T(8,128)} %adjoint_steps.1) | data formatting | bytes 65536

commit v3 on v2

--- a/solution.py
+++ b/solution.py
@@ -47,6 +47,12 @@
     inner, outer, far, behind = at(-1), at(1), at(2), at(-2)
     others = [lax.rem(tracer + j, tracers_n) for j in range(1, tracers_n)]
 
+    barrier = pltpu.get_barrier_semaphore()
+    for device in (inner, outer, far, behind):
+        pl.semaphore_signal(barrier, inc=1, device_id={"region": device}, device_id_type=MESH)
+    for other in others:
+        pl.semaphore_signal(barrier, inc=1, device_id={"tracer": other}, device_id_type=MESH)
+
     loads = [
         pltpu.make_async_copy(src, dst, load_sem.at[k])
         for k, (src, dst) in enumerate(
@@ -62,13 +68,6 @@
     for copy in own_states[::-1]:
         copy.start()
 
-    barrier = pltpu.get_barrier_semaphore()
-    for device in (inner, outer, behind):
-        pl.semaphore_signal(barrier, inc=1, device_id={"region": device}, device_id_type=MESH)
-    for other in others:
-        pl.semaphore_signal(barrier, inc=1, device_id={"tracer": other}, device_id_type=MESH)
-    pl.semaphore_wait(barrier, 3 + len(others))
-
     def state_copy(n, j):
         return pltpu.make_async_remote_copy(
             src_ref=states_hbm.at[n],
@@ -91,7 +90,7 @@
 
     def region_copy(i, k):
         src, dst, target = (
-            (relay_out, relay_in, inner),
+            (relay_out, relay_in, behind),
             (direct_out, direct_in, far),
             (peer_out, peer_in, inner),
             (merged_out, merged_in, outer),
@@ -106,9 +105,6 @@
         )
 
     peers = range(len(others))
-    for n in range(steps - 1, max(steps - 3, -1), -1):
-        for j in peers:
-            state_copy(n, j).start()
 
     lane = lax.broadcasted_iota(jnp.int32, (1, boxes), 1)
     wet_of = jnp.zeros((1, boxes), jnp.int32)
@@ -183,44 +179,57 @@
         bent = jnp.tanh(dot_split(uptake, joined(full_state, n)))
         gain[...] = 1.0 - bent * bent
 
-    def step(i, carry):
+    def step(i, first):
         n = steps - 1 - i
         settled = settle(adj[...])
         full_settled[i, tracer] = settled
-        for j in peers:
-            settled_copy(i, j).start()
         half = settled.astype(BF16)
-
-        @pl.when(i == 0)
-        def _():
-            loads[4].wait()
 
         def term(distance):
             slot, live = places[distance]
             return dot(half, tiles[slot]) * live
 
-        relay_out[i] = term(-2)
-        region_copy(i, 0).start()
-        direct_out[i] = term(2)
-        region_copy(i, 1).start()
-        near = term(1)
-        region_copy(i, 0).wait_recv()
-        merged_out[i] = near + relay_in[i]
-        region_copy(i, 3).start()
-        peer_out[i] = term(-1)
-        region_copy(i, 2).start()
+        def send_settled():
+            for j in peers:
+                settled_copy(i, j).start()
+
+        if first:
+            loads[4].wait()
+            relay_out[i] = term(-2)
+            direct_out[i] = term(2)
+            peer_out[i] = term(-1)
+            merged_out[i] = term(1)
+            total = term(0)
+            pl.semaphore_wait(barrier, 4 + len(others))
+            region_copy(i, 0).start()
+            region_copy(i, 1).start()
+            region_copy(i, 3).start()
+            for j in peers:
+                state_copy(n, j).start()
+            send_settled()
+            region_copy(i, 2).start()
+            if steps > 1:
+                for j in peers:
+                    state_copy(n - 1, j).start()
+        else:
+            send_settled()
+            relay_out[i] = term(-2)
+            region_copy(i, 0).start()
+            direct_out[i] = term(2)
+            region_copy(i, 1).start()
+            merged_out[i] = term(1)
+            region_copy(i, 3).start()
+            peer_out[i] = term(-1)
+            region_copy(i, 2).start()
+            total = term(0)
 
         @pl.when(n >= 2)
         def _():
             for j in peers:
                 state_copy(n - 2, j).start()
 
-        total = term(0)
-
-        @pl.when(i == 0)
-        def _():
+        if first:
             make_gain(n)
-
         for j in peers:
             settled_copy(i, j).wait_recv()
         weighted = gain[...] * dot_split(release, joined(full_settled, i))
@@ -235,10 +244,16 @@
         region_copy(i, 1).wait_recv()
         total = total + direct_in[i]
         region_copy(i, 3).wait_recv()
-        adj[...] = wet_mask * (total + merged_in[i])
+        total = total + merged_in[i]
+        region_copy(i, 0).wait_recv()
+        adj[...] = wet_mask * (total + relay_in[i])
+
+    def later_step(i, carry):
+        step(i, False)
         return carry
 
-    lax.fori_loop(0, steps, step, 0)
+    step(0, True)
+    lax.fori_loop(1, steps, later_step, 0)
     out[...] = adj[...]
 
     def drain(i, carry):

time: 40.5 us -> 39.8 us (0.983)
  Pallas kernels: 38.3 us -> 37.5 us
    pallas_call x1, Pallas kernels: 38.3 us -> 37.5 us  [local(): pl.pallas_call(kernel, out_shape=jax.ShapeDtypeStruct((tr, boxes), F32),...]
where the time goes in v3:
time: 39.8 us; the launch traced here: 39.6 us
  Pallas kernels  37.5 us (94%)
  local copies, waits for them, and re-layouts  1.38 us (3%)
  between operations  0.66 us (2%)
    pallas_call x1, Pallas kernels, local(): pl.pallas_call(kernel, out_shape=jax.ShapeDtypeStruct((tr, boxes), F32),...  37.5 us
    unnamed x1, local copies, waits for them, and re-layouts  1.38 us

profile of v3, /device:TPU:0, one launch (start us, length us, event | category | flops | bytes accessed | tf_op | source)
XLA Modules:
  0.0 39.6 jit_solution(9615078104592608360)
XLA Ops:
  0.7 37.5 %adjoint_steps.1 = f32[16,512]{1,0:T(8,128)} custom-call(f32[16,512]{1,0:T(8,128)} %cot_hbm.1, f32[6,16,512]{2,1,0:T(8,128)} %states_hbm.1, f32[16,32,32]{2,1,0:T(8,128)} %inv_hbm.1, s32[16]{0:T(128)} %wet.1, bf16[1,5,512,512]{3,2,1,0:T(8,128)(2,1)} %tiles_hbm.1, s32[1,5]{1,0:T(1,128)} %off.1, s32[1]{0:T(128)S(6)} %copy.11.cnt, f32[32,32]{1,0:T(8,128)} %up_hbm.1, ...), custom_call_target="tpu_custom_call" | custom-call | tf_op jit(solution)/shard_map/adjoint_steps/pallas_call | solution.py:292
  38.2 1.4 %copy.12 = f32[16,512]{1,0:T(8,128)} copy(f32[16,512]{1,0:T(8,128)} %adjoint_steps.1) | data formatting | bytes 65536

commit v4 on v3

--- a/solution.py
+++ b/solution.py
@@ -213,10 +213,10 @@
                     state_copy(n - 1, j).start()
         else:
             send_settled()
+            direct_out[i] = term(2)
+            region_copy(i, 1).start()
             relay_out[i] = term(-2)
             region_copy(i, 0).start()
-            direct_out[i] = term(2)
-            region_copy(i, 1).start()
             merged_out[i] = term(1)
             region_copy(i, 3).start()
             peer_out[i] = term(-1)
@@ -228,16 +228,11 @@
             for j in peers:
                 state_copy(n - 2, j).start()
 
-        if first:
-            make_gain(n)
+        make_gain(n)
         for j in peers:
             settled_copy(i, j).wait_recv()
         weighted = gain[...] * dot_split(release, joined(full_settled, i))
         total = total + dot_split(uptake_own, weighted)
-
-        @pl.when(n >= 1)
-        def _():
-            make_gain(n - 1)
 
         region_copy(i, 2).wait_recv()
         total = total + peer_in[i]

time: 39.8 us -> 39.1 us (0.982)
  Pallas kernels: 37.5 us -> 36.8 us
    pallas_call x1, Pallas kernels: 37.5 us -> 36.8 us  [local(): pl.pallas_call(kernel, out_shape=jax.ShapeDtypeStruct((tr, boxes), F32),...]
where the time goes in v4:
time: 39.1 us; the launch traced here: 38.9 us
  Pallas kernels  36.8 us (94%)
  local copies, waits for them, and re-layouts  1.38 us (4%)
  between operations  0.66 us (2%)
    pallas_call x1, Pallas kernels, local(): pl.pallas_call(kernel, out_shape=jax.ShapeDtypeStruct((tr, boxes), F32),...  36.8 us
    unnamed x1, local copies, waits for them, and re-layouts  1.38 us

profile of v4, /device:TPU:0, one launch (start us, length us, event | category | flops | bytes accessed | tf_op | source)
XLA Modules:
  0.0 38.9 jit_solution(15895055870766814511)
XLA Ops:
  0.7 36.8 %adjoint_steps.1 = f32[16,512]{1,0:T(8,128)} custom-call(f32[16,512]{1,0:T(8,128)} %cot_hbm.1, f32[6,16,512]{2,1,0:T(8,128)} %states_hbm.1, f32[16,32,32]{2,1,0:T(8,128)} %inv_hbm.1, s32[16]{0:T(128)} %wet.1, bf16[1,5,512,512]{3,2,1,0:T(8,128)(2,1)} %tiles_hbm.1, s32[1,5]{1,0:T(1,128)} %off.1, s32[1]{0:T(128)S(6)} %copy.11.cnt, f32[32,32]{1,0:T(8,128)} %up_hbm.1, ...), custom_call_target="tpu_custom_call" | custom-call | tf_op jit(solution)/shard_map/adjoint_steps/pallas_call | solution.py:287
  37.5 1.4 %copy.12 = f32[16,512]{1,0:T(8,128)} copy(f32[16,512]{1,0:T(8,128)} %adjoint_steps.1) | data formatting | bytes 65536

commit v5 on v4

--- a/solution.py
+++ b/solution.py
@@ -178,6 +178,13 @@
         pltpu.make_async_copy(states_hbm.at[n], full_state.at[n, tracer], own_sem.at[n]).wait()
         bent = jnp.tanh(dot_split(uptake, joined(full_state, n)))
         gain[...] = 1.0 - bent * bent
+
+    def drain(i):
+        for k in range(4):
+            region_copy(i, k).wait_send()
+        for j in peers:
+            settled_copy(i, j).wait_send()
+            state_copy(steps - 1 - i, j).wait_send()
 
     def step(i, first):
         n = steps - 1 - i
@@ -212,9 +219,9 @@
                 for j in peers:
                     state_copy(n - 1, j).start()
         else:
-            send_settled()
             direct_out[i] = term(2)
             region_copy(i, 1).start()
+            send_settled()
             relay_out[i] = term(-2)
             region_copy(i, 0).start()
             merged_out[i] = term(1)
@@ -228,6 +235,8 @@
             for j in peers:
                 state_copy(n - 2, j).start()
 
+        if not first:
+            drain(i - 1)
         make_gain(n)
         for j in peers:
             settled_copy(i, j).wait_recv()
@@ -250,16 +259,7 @@
     step(0, True)
     lax.fori_loop(1, steps, later_step, 0)
     out[...] = adj[...]
-
-    def drain(i, carry):
-        for k in range(4):
-            region_copy(i, k).wait_send()
-        for j in peers:
-            settled_copy(i, j).wait_send()
-            state_copy(i, j).wait_send()
-        return carry
-
-    lax.fori_loop(0, steps, drain, 0)
+    drain(steps - 1)
 
 
 def local(

time: 39.1 us -> 38.8 us (level)
  no operation moved by 1% of the time
where the time goes in v5:
time: 38.8 us; the launch traced here: 38.6 us
  Pallas kernels  36.5 us (94%)
  local copies, waits for them, and re-layouts  1.38 us (4%)
  between operations  0.66 us (2%)
    pallas_call x1, Pallas kernels, local(): pl.pallas_call(kernel, out_shape=jax.ShapeDtypeStruct((tr, boxes), F32),...  36.5 us
    unnamed x1, local copies, waits for them, and re-layouts  1.38 us

profile of v5, /device:TPU:0, one launch (start us, length us, event | category | flops | bytes accessed | tf_op | source)
XLA Modules:
  0.0 38.6 jit_solution(4487152868076377540)
XLA Ops:
  0.7 36.5 %adjoint_steps.1 = f32[16,512]{1,0:T(8,128)} custom-call(f32[16,512]{1,0:T(8,128)} %cot_hbm.1, f32[6,16,512]{2,1,0:T(8,128)} %states_hbm.1, f32[16,32,32]{2,1,0:T(8,128)} %inv_hbm.1, s32[16]{0:T(128)} %wet.1, bf16[1,5,512,512]{3,2,1,0:T(8,128)(2,1)} %tiles_hbm.1, s32[1,5]{1,0:T(1,128)} %off.1, s32[1]{0:T(128)S(6)} %copy.11.cnt, f32[32,32]{1,0:T(8,128)} %up_hbm.1, ...), custom_call_target="tpu_custom_call" | custom-call | tf_op jit(solution)/shard_map/adjoint_steps/pallas_call | solution.py:287
  37.2 1.4 %copy.12 = f32[16,512]{1,0:T(8,128)} copy(f32[16,512]{1,0:T(8,128)} %adjoint_steps.1) | data formatting | bytes 65536

commit v6 on v5

--- a/solution.py
+++ b/solution.py
@@ -24,7 +24,10 @@
 
 def dot_split(a, b):
     (a_high, a_low), (b_high, b_low) = a, halves(b)
-    return dot(a_high, b_high) + (dot(a_high, b_low) + dot(a_low, b_high))
+    return dot(
+        jnp.concatenate([a_high, a_high, a_low], axis=1),
+        jnp.concatenate([b_high, b_low, b_high], axis=0),
+    )
 
 
 def kernel(
@@ -208,12 +211,12 @@
             merged_out[i] = term(1)
             total = term(0)
             pl.semaphore_wait(barrier, 4 + len(others))
+            for j in peers:
+                state_copy(n, j).start()
+            send_settled()
             region_copy(i, 0).start()
             region_copy(i, 1).start()
             region_copy(i, 3).start()
-            for j in peers:
-                state_copy(n, j).start()
-            send_settled()
             region_copy(i, 2).start()
             if steps > 1:
                 for j in peers:

time: 38.8 us -> 38.8 us (level)
  no operation moved by 1% of the time
where the time goes in v6:
time: 38.8 us; the launch traced here: 38.6 us
  Pallas kernels  36.5 us (94%)
  local copies, waits for them, and re-layouts  1.38 us (4%)
  between operations  0.66 us (2%)
    pallas_call x1, Pallas kernels, local(): pl.pallas_call(kernel, out_shape=jax.ShapeDtypeStruct((tr, boxes), F32),...  36.5 us
    unnamed x1, local copies, waits for them, and re-layouts  1.38 us

profile of v6, /device:TPU:0, one launch (start us, length us, event | category | flops | bytes accessed | tf_op | source)
XLA Modules:
  0.0 38.6 jit_solution(9341364180637876270)
XLA Ops:
  0.7 36.5 %adjoint_steps.1 = f32[16,512]{1,0:T(8,128)} custom-call(f32[16,512]{1,0:T(8,128)} %cot_hbm.1, f32[6,16,512]{2,1,0:T(8,128)} %states_hbm.1, f32[16,32,32]{2,1,0:T(8,128)} %inv_hbm.1, s32[16]{0:T(128)} %wet.1, bf16[1,5,512,512]{3,2,1,0:T(8,128)(2,1)} %tiles_hbm.1, s32[1,5]{1,0:T(1,128)} %off.1, s32[1]{0:T(128)S(6)} %copy.11.cnt, f32[32,32]{1,0:T(8,128)} %up_hbm.1, ...), custom_call_target="tpu_custom_call" | custom-call | tf_op jit(solution)/shard_map/adjoint_steps/pallas_call | solution.py:290
  37.2 1.4 %copy.12 = f32[16,512]{1,0:T(8,128)} copy(f32[16,512]{1,0:T(8,128)} %adjoint_steps.1) | data formatting | bytes 65536
